TPU v7x, 256 devices: a whole 4x4x8 slice. The times are simulated.
256 devices in a mesh: date: 128 (over x, y, z), col: 2 (over core).
Axes of the slice: x: 4, y: 4, z: 8, core: 2. Of those that a mesh axis runs over, the one named last changes fastest.
Arguments:
- slc: bfloat16 [2, 256, 16, 4096], P(None, 'date', None, 'col'), may hold values from -6 to 6
- partner_offsets: int32 [256, 24], replicated, may hold values from 0 to 50, as said below
Outputs:
- linked: float32 [2, 4, 256, 256], P(None, None, ('date', 'col'))
Inputs may be any that keep to these rules, and one draw needn't show every extreme that they name: `partner_offsets`: live slots of a date come first; its live offsets are distinct and lead to dates inside the stack; some date has 24 live slots, and the largest possible offset is used.
All inputs are finite; a program needn't handle non-finite values.
Results may differ from a plain program's by a relative error of at most 0.00045.
Values may be sent and summed in bfloat16 or wider, within the bound.
A program may use at most 128 MiB of HBM per device.

v0:
```python
import jax
import jax.numpy as jnp
from jax import lax
from jax.sharding import PartitionSpec as P

WIN = 50
ITERS = 20


epsilon = 1e-06
highest = lax.Precision.HIGHEST


def passed_along(value, axis, by):
    length = lax.axis_size(axis)
    pairs = [(i, i + by) for i in range(length) if 0 <= i + by < length]
    return lax.ppermute(value, axis, pairs)


def boxcar_matrix(col_count):
    column_index = jnp.arange(col_count, dtype=jnp.int32)[:, None] // 16
    looked_index = jnp.arange(col_count // 16, dtype=jnp.int32)[None, :]
    return jnp.where(column_index == looked_index, 1.0, 0.0).astype(jnp.float32)


def box_mean(values, boxcar):
    layout = values.shape
    row_sums = jnp.sum(values.reshape(layout[:-2] + (layout[-2] // 4, 4, layout[-1])), axis=-2)
    return jnp.matmul(row_sums, boxcar, precision=highest) / 64.0


def power_link(upper_real, upper_imag):
    date_count = upper_real.shape[-1]
    identity = jnp.eye(date_count, dtype=jnp.float32)
    herm_real = identity + upper_real + jnp.swapaxes(upper_real, -1, -2)
    herm_imag = upper_imag - jnp.swapaxes(upper_imag, -1, -2)
    start_real = jnp.ones(upper_real.shape[:-1], jnp.float32)
    start_imag = jnp.zeros(upper_real.shape[:-1], jnp.float32)

    def advance(counter, vector):
        vec_real, vec_imag = vector
        new_real = jnp.einsum(
            "...ij,...j->...i", herm_real, vec_real, precision=highest
        ) - jnp.einsum("...ij,...j->...i", herm_imag, vec_imag, precision=highest)
        new_imag = jnp.einsum(
            "...ij,...j->...i", herm_real, vec_imag, precision=highest
        ) + jnp.einsum("...ij,...j->...i", herm_imag, vec_real, precision=highest)
        factor = lax.rsqrt(
            jnp.mean(new_real * new_real + new_imag * new_imag, axis=-1, keepdims=True) + epsilon
        )
        return (new_real * factor, new_imag * factor)

    return lax.fori_loop(0, ITERS, advance, (start_real, start_imag))


def on_device(slc, partner_offsets):
    own_count = slc.shape[1]
    row_count = slc.shape[2]
    col_count = slc.shape[3]
    date_groups = lax.axis_size("date")
    core_groups = lax.axis_size("col")
    date_count = own_count * date_groups
    looked_rows = row_count // 4
    looked_cols = col_count // 16
    block_cols = looked_cols // date_groups
    outer_blocks = date_groups // core_groups
    pixel_count = looked_rows * block_cols
    slot_count = partner_offsets.shape[1]
    all_live = partner_offsets > 0
    all_target = jnp.arange(date_count, dtype=jnp.int32)[:, None] + partner_offsets
    onehot = jnp.where(
        all_live[:, :, None]
        & (all_target[:, :, None] == jnp.arange(date_count, dtype=jnp.int32)[None, None, :]),
        1.0,
        0.0,
    ).astype(jnp.float32)
    boxcar = boxcar_matrix(col_count)
    first_date = lax.axis_index("date") * own_count
    own_offsets = lax.dynamic_slice_in_dim(partner_offsets, first_date, own_count, 0)
    own_live = own_offsets > 0
    own_target = first_date + jnp.arange(own_count, dtype=jnp.int32)[:, None] + own_offsets
    own_float = slc.astype(jnp.float32)
    own_power = box_mean(own_float[0] * own_float[0] + own_float[1] * own_float[1], boxcar)

    def absorb(totals, tile, base_date):
        total_real, total_imag = totals
        tile_float = tile.astype(jnp.float32)
        tile_power = box_mean(tile_float[0] * tile_float[0] + tile_float[1] * tile_float[1], boxcar)
        numer_real = box_mean(
            own_float[0][:, None] * tile_float[0][None]
            + own_float[1][:, None] * tile_float[1][None],
            boxcar,
        )
        numer_imag = box_mean(
            own_float[1][:, None] * tile_float[0][None]
            - own_float[0][:, None] * tile_float[1][None],
            boxcar,
        )
        denom = jnp.sqrt((own_power[:, None] + epsilon) * (tile_power[None] + epsilon))
        pair_real = numer_real / denom
        pair_imag = numer_imag / denom
        for member in range(tile.shape[1]):
            chosen = (own_live & (own_target == base_date + member))[:, :, None, None]
            total_real = total_real + jnp.where(chosen, pair_real[:, member][:, None], 0.0)
            total_imag = total_imag + jnp.where(chosen, pair_imag[:, member][:, None], 0.0)
        return (total_real, total_imag)

    empty = jnp.zeros((own_count, slot_count, looked_rows, looked_cols), jnp.float32)
    totals = absorb((empty, empty), slc, first_date)
    reach = (WIN + own_count - 1) // own_count
    for distance in range(1, reach + 1):
        tile = passed_along(slc, "date", -distance)
        totals = absorb(totals, tile, first_date + distance * own_count)
    coherence = jnp.stack(totals).reshape(2, own_count, slot_count * looked_rows, looked_cols)
    coherence = jnp.transpose(coherence, (0, 1, 3, 2))
    coherence = coherence.reshape(
        2, own_count, 1, outer_blocks, core_groups, block_cols * slot_count * looked_rows
    )
    on_cores = lax.all_to_all(coherence, "col", split_axis=4, concat_axis=2, tiled=True)
    on_cores = on_cores.reshape(2, own_count, date_groups, block_cols * slot_count * looked_rows)
    on_pixels = lax.all_to_all(on_cores, "date", split_axis=2, concat_axis=1, tiled=True)
    slots = on_pixels.reshape(2, date_count, block_cols, slot_count, looked_rows)
    upper_real = jnp.einsum("ibkl,ikj->lbij", slots[0], onehot, precision=highest).reshape(
        pixel_count, date_count, date_count
    )
    upper_imag = jnp.einsum("ibkl,ikj->lbij", slots[1], onehot, precision=highest).reshape(
        pixel_count, date_count, date_count
    )
    vec_real, vec_imag = power_link(upper_real, upper_imag)
    linked = jnp.stack([vec_real, vec_imag]).reshape(2, looked_rows, block_cols, date_count)
    return linked


def solution(mesh):
    return jax.shard_map(
        on_device,
        mesh=mesh,
        in_specs=(P(None, "date", None, "col"), P()),
        out_specs=P(None, None, ("date", "col"), None),
        check_vma=False,
    )
```

profile of v0, /device:TPU:1, one launch (start us, length us, event | category | flops | bytes accessed | tf_op | source)
XLA Modules:
  0.0 529.5 jit_solution(5660686011113917641)
XLA Ops:
  62.1 3.5 collective-permute-done.5
  68.4 10.3 %collective-permute-done.6 = bf16[2,2,16,2048]{3,2,1,0:T(8,128)(2,1)S(1)} collective-permute-done((bf16[2,2,16,2048]{3,2,1,0:T(8,128)(2,1)}, bf16[2,2,16,2048]{3,2,1,0:T(8,128)(2,1)S(1)}, u32[]{:S(2)}, u32[]{:S(2)}) %collective-permute-start.6) | collective-permute-done | bytes 262176 | tf_op jit(solution)/shard_map/ppermute | solution.py:17
  87.6 23.0 %collective-permute-done.10 = bf16[2,2,16,2048]{3,2,1,0:T(8,128)(2,1)S(1)} collective-permute-done((bf16[2,2,16,2048]{3,2,1,0:T(8,128)(2,1)}, bf16[2,2,16,2048]{3,2,1,0:T(8,128)(2,1)S(1)}, u32[]{:S(2)}, u32[]{:S(2)}) %collective-permute-start.10) | collective-permute-done | bytes 262176 | tf_op jit(solution)/shard_map/ppermute | solution.py:17
  119.5 8.2 %collective-permute-done.13 = bf16[2,2,16,2048]{3,2,1,0:T(8,128)(2,1)S(1)} collective-permute-done((bf16[2,2,16,2048]{3,2,1,0:T(8,128)(2,1)}, bf16[2,2,16,2048]{3,2,1,0:T(8,128)(2,1)S(1)}, u32[]{:S(2)}, u32[]{:S(2)}) %collective-permute-start.13) | collective-permute-done | bytes 262176 | tf_op jit(solution)/shard_map/ppermute | solution.py:17
  130.8 1.7 mul.2128
  132.5 15.0 %collective-permute-done.14 = bf16[2,2,16,2048]{3,2,1,0:T(8,128)(2,1)} collective-permute-done((bf16[2,2,16,2048]{3,2,1,0:T(8,128)(2,1)}, bf16[2,2,16,2048]{3,2,1,0:T(8,128)(2,1)}, u32[]{:S(2)}, u32[]{:S(2)}) %collective-permute-start.14) | collective-permute-done | bytes 262176 | tf_op jit(solution)/shard_map/ppermute | solution.py:17
  148.8 1.8 fusion.668
  150.6 1.7 mul.2135
  155.4 1.8 fusion.667
  158.9 1.7 mul.2148
  161.9 1.8 fusion.675
  165.4 1.7 mul.2228
  168.5 1.8 fusion.682
  170.3 1.7 mul.2155
  175.0 1.8 fusion.681
  176.8 1.7 mul.2165
  178.6 1.7 mul.2168
  180.3 14.2 %collective-permute-start.24 = (bf16[2,2,16,2048]{3,2,1,0:T(8,128)(2,1)}, bf16[2,2,16,2048]{3,2,1,0:T(8,128)(2,1)}, u32[]{:S(2)}, u32[]{:S(2)}) collective-permute-start(bf16[2,2,16,2048]{3,2,1,0:T(8,128)(2,1)} %param.4), channel_id=1, source_target_pairs={{50,0},{52,2},{54,4},{56,6},{58,8},{60,10},{62,12},{64,14},{66,16}... | collective-permute-start | bytes 786440 | tf_op jit(solution)/shard_map/ppermute | solution.py:17
  194.5 1.8 fusion.680
  199.7 1.8 fusion.679
  201.5 1.7 mul.2185
  203.3 1.7 mul.2188
  205.0 1.8 fusion.678
  210.3 2.0 add_reduce_fusion.51
  212.4 1.9 add_reduce_fusion.50
  214.2 1.9 add_reduce_fusion.49
  216.1 1.9 add_reduce_fusion.48
  218.0 1.9 add_reduce_fusion.47
  219.9 1.9 add_reduce_fusion.46
  221.9 9.7 %add_reduce_fusion.25 = (f32[2,2,4,2048]{3,2,1,0:T(4,128)}, f32[2,2,4,2048]{3,2,1,0:T(4,128)}, f32[2,2,4,2048]{3,2,1,0:T(4,128)}, f32[2,2,4,2048]{3,2,1,0:T(4,12...) fusion(f32[2,4,4,2048]{3,2,1,0:T(4,128)S(1)} %copy-done.22, ...), kind=kLoop, calls=%fused_computation.320 | loop fusion | flops 8847360 | bytes 7077888 | tf_op jit(solution)/shard_map/reduce_sum | solution.py:28
  233.2 1.8 fusion.677
  235.0 1.7 mul.2205
  242.7 1.8 add_reduce_fusion.38
  244.5 7.9 %add_reduce_fusion.17 = (f32[2,2,4,2048]{3,2,1,0:T(4,128)}, f32[2,2,4,2048]{3,2,1,0:T(4,128)}, f32[2,2,4,2048]{3,2,1,0:T(4,128)}, f32[2,2,4,2048]{3,2,1,0:T(4,12...) fusion(f32[2,4,4,2048]{3,2,1,0:T(4,128)S(1)} %mul.2078, ...), kind=kLoop, calls=%fused_computation.312 | loop fusion | flops 7864320 | bytes 6815744 | tf_op jit(solution)/shard_map/reduce_sum | solution.py:28
  254.1 1.8 fusion.676
  255.9 1.7 mul.2215
  263.6 1.8 add_reduce_fusion.31
  265.5 8.2 %add_reduce_fusion.9 = (f32[2,2,4,2048]{3,2,1,0:T(4,128)}, f32[2,2,4,2048]{3,2,1,0:T(4,128)}, f32[2,2,4,2048]{3,2,1,0:T(4,128)}, f32[2,2,4,2048]{3,2,1,0:T(4,128...) fusion(f32[2,4,4,2048]{3,2,1,0:T(4,128)S(1)} %copy-done.6, ...), kind=kLoop, calls=%fused_computation.304 | loop fusion | flops 7864320 | bytes 6815744 | tf_op jit(solution)/shard_map/reduce_sum | solution.py:28
  348.7 3.5 select_add_fusion.1
  353.6 2.3 select_add_fusion
  356.1 5.0 all_to_all.30
  362.1 40.3 %all-to-all-start.1 = ((f32[2,2,128,96]{3,1,0,2:T(2,128)}), f32[2,2,128,96]{3,1,0,2:T(2,128)S(1)}, u32[]{:S(2)}, u32[]{:S(2)}) async-start(f32[2,2,128,96]{3,1,0,2:T(2,128)} %copy.426), calls=%async_computation.1 | async-start | bytes 524288 | tf_op jit(solution)/shard_map/all_to_all | solution.py:121
  402.7 13.7 %all-to-all-done.1 = f32[2,2,128,96]{3,1,0,2:T(2,128)S(1)} async-done(((f32[2,2,128,96]{3,1,0,2:T(2,128)}), f32[2,2,128,96]{3,1,0,2:T(2,128)S(1)}, u32[]{:S(2)}, u32[]{:S(2)}) %all-to-all-start.1) | async-done | bytes 196640 | tf_op jit(solution)/shard_map/all_to_all | solution.py:121
  416.5 2.7 reshape.2412
  419.2 9.0 %fusion.101 = f32[4,256,256]{2,0,1:T(4,128)S(1)} fusion(f32[256,24,4]{2,1,0:T(8,128)} %reshape.2412, s32[256,24]{1,0:T(8,128)S(1)} %copy.421, pred[256,24]{1,0:T(8,128)(4,1)S(1)} %copy.420), kind=kOutput, calls=%fused_computation.110 | convolution fusion | flops 80216064 | bytes 1177600 | tf_op jit(solution)/shard_map/ibkl,ikj->lbij/dot_general | solution.py:126
  429.4 2.7 reshape.2410
  432.1 9.0 %fusion.10 = f32[256,256,4]{1,2,0:T(4,128)S(1)} fusion(f32[256,24,4]{2,1,0:T(8,128)} %reshape.2410, s32[256,24]{1,0:T(8,128)S(1)} %copy.421, pred[256,24]{1,0:T(8,128)(4,1)S(1)} %copy.420), kind=kOutput, calls=%fused_computation.18 | convolution fusion | flops 80216064 | bytes 1177600 | tf_op jit(solution)/shard_map/ibkl,ikj->lbij/dot_general | solution.py:123
  444.5 83.9 %while.13 = (s32[]{:T(128)}, f32[4,256]{1,0:T(4,128)S(1)}, f32[4,256]{1,0:T(4,128)S(1)}, f32[4,256,256]{2,1,0:T(8,128)S(1)}, f32[4,256,256]{2,1,0:T(8,128)S(1)}, /*index=5*/s32[]{:T(128)}, s32[]{:T(128)}) while((s32[]{:T(128)}, f32[4,256]{1,0:T(4,128)S(1)}, f32[4,256]{1,0:T(4,128)S(1)}, f32[4,256,256]{2,1,0:T(8,128)S(1)}, ...), condition=%wide.region_80.81_spmd.clone, body=%wide.region_78.80_spmd.clone.sunk | while | flops 12595207 | bytes 4284567 | solution.py:53
  (967 shorter events, 284.3 us)
Async XLA Ops:
  0.0 47.5 %collective-permute-start = (bf16[2,2,16,2048]{3,2,1,0:T(8,128)(2,1)}, bf16[2,2,16,2048]{3,2,1,0:T(8,128)(2,1)S(1)}, u32[]{:S(2)}, u32[]{:S(2)}) collective-permute-start(bf16[2,2,16,2048]{3,2,1,0:T(8,128)(2,1)} %param.4), channel_id=1, source_target_pairs={{2,0},{4,2},{6,4},{8,6},{10,8},{12,10},{14,12},{16,14},{18,16},{20... | collective-permute-start | bytes 786440 | tf_op jit(solution)/shard_map/ppermute | solution.py:17
  1.3 49.1 %collective-permute-start.1 = (bf16[2,2,16,2048]{3,2,1,0:T(8,128)(2,1)}, bf16[2,2,16,2048]{3,2,1,0:T(8,128)(2,1)S(1)}, u32[]{:S(2)}, u32[]{:S(2)}) collective-permute-start(bf16[2,2,16,2048]{3,2,1,0:T(8,128)(2,1)} %param.4), channel_id=1, source_target_pairs={{4,0},{6,2},{8,4},{10,6},{12,8},{14,10},{16,12},{18,14},{20,16},{2... | collective-permute-start | bytes 786440 | tf_op jit(solution)/shard_map/ppermute | solution.py:17
  2.6 50.7 %collective-permute-start.2 = (bf16[2,2,16,2048]{3,2,1,0:T(8,128)(2,1)}, bf16[2,2,16,2048]{3,2,1,0:T(8,128)(2,1)S(1)}, u32[]{:S(2)}, u32[]{:S(2)}) collective-permute-start(bf16[2,2,16,2048]{3,2,1,0:T(8,128)(2,1)} %param.4), channel_id=1, source_target_pairs={{6,0},{8,2},{10,4},{12,6},{14,8},{16,10},{18,12},{20,14},{22,16},{... | collective-permute-start | bytes 786440 | tf_op jit(solution)/shard_map/ppermute | solution.py:17
  3.9 52.3 %collective-permute-start.3 = (bf16[2,2,16,2048]{3,2,1,0:T(8,128)(2,1)}, bf16[2,2,16,2048]{3,2,1,0:T(8,128)(2,1)S(1)}, u32[]{:S(2)}, u32[]{:S(2)}) collective-permute-start(bf16[2,2,16,2048]{3,2,1,0:T(8,128)(2,1)} %param.4), channel_id=1, source_target_pairs={{8,0},{10,2},{12,4},{14,6},{16,8},{18,10},{20,12},{22,14},{24,16},... | collective-permute-start | bytes 786440 | tf_op jit(solution)/shard_map/ppermute | solution.py:17
  5.2 54.0 %collective-permute-start.4 = (bf16[2,2,16,2048]{3,2,1,0:T(8,128)(2,1)}, bf16[2,2,16,2048]{3,2,1,0:T(8,128)(2,1)S(1)}, u32[]{:S(2)}, u32[]{:S(2)}) collective-permute-start(bf16[2,2,16,2048]{3,2,1,0:T(8,128)(2,1)} %param.4), channel_id=1, source_target_pairs={{10,0},{12,2},{14,4},{16,6},{18,8},{20,10},{22,12},{24,14},{26,16}... | collective-permute-start | bytes 786440 | tf_op jit(solution)/shard_map/ppermute | solution.py:17
  47.5 18.0 %collective-permute-start.5 = (bf16[2,2,16,2048]{3,2,1,0:T(8,128)(2,1)}, bf16[2,2,16,2048]{3,2,1,0:T(8,128)(2,1)S(1)}, u32[]{:S(2)}, u32[]{:S(2)}) collective-permute-start(bf16[2,2,16,2048]{3,2,1,0:T(8,128)(2,1)} %param.4), channel_id=1, source_target_pairs={{12,0},{14,2},{16,4},{18,6},{20,8},{22,10},{24,12},{26,14},{28,16}... | collective-permute-start | bytes 786440 | tf_op jit(solution)/shard_map/ppermute | solution.py:17
  50.4 28.4 %collective-permute-start.6 = (bf16[2,2,16,2048]{3,2,1,0:T(8,128)(2,1)}, bf16[2,2,16,2048]{3,2,1,0:T(8,128)(2,1)S(1)}, u32[]{:S(2)}, u32[]{:S(2)}) collective-permute-start(bf16[2,2,16,2048]{3,2,1,0:T(8,128)(2,1)} %param.4), channel_id=1, source_target_pairs={{14,0},{16,2},{18,4},{20,6},{22,8},{24,10},{26,12},{28,14},{30,16}... | collective-permute-start | bytes 786440 | tf_op jit(solution)/shard_map/ppermute | solution.py:17
  53.3 28.3 %collective-permute-start.7 = (bf16[2,2,16,2048]{3,2,1,0:T(8,128)(2,1)}, bf16[2,2,16,2048]{3,2,1,0:T(8,128)(2,1)S(1)}, u32[]{:S(2)}, u32[]{:S(2)}) collective-permute-start(bf16[2,2,16,2048]{3,2,1,0:T(8,128)(2,1)} %param.4), channel_id=1, source_target_pairs={{16,0},{18,2},{20,4},{22,6},{24,8},{26,10},{28,12},{30,14},{32,16}... | collective-permute-start | bytes 786440 | tf_op jit(solution)/shard_map/ppermute | solution.py:17
  56.2 28.4 %collective-permute-start.8 = (bf16[2,2,16,2048]{3,2,1,0:T(8,128)(2,1)}, bf16[2,2,16,2048]{3,2,1,0:T(8,128)(2,1)S(1)}, u32[]{:S(2)}, u32[]{:S(2)}) collective-permute-start(bf16[2,2,16,2048]{3,2,1,0:T(8,128)(2,1)} %param.4), channel_id=1, source_target_pairs={{18,0},{20,2},{22,4},{24,6},{26,8},{28,10},{30,12},{32,14},{34,16}... | collective-permute-start | bytes 786440 | tf_op jit(solution)/shard_map/ppermute | solution.py:17
  59.1 26.9 %collective-permute-start.9 = (bf16[2,2,16,2048]{3,2,1,0:T(8,128)(2,1)}, bf16[2,2,16,2048]{3,2,1,0:T(8,128)(2,1)S(1)}, u32[]{:S(2)}, u32[]{:S(2)}) collective-permute-start(bf16[2,2,16,2048]{3,2,1,0:T(8,128)(2,1)} %param.4), channel_id=1, source_target_pairs={{20,0},{22,2},{24,4},{26,6},{28,8},{30,10},{32,12},{34,14},{36,16}... | collective-permute-start | bytes 786440 | tf_op jit(solution)/shard_map/ppermute | solution.py:17
  65.5 45.1 %collective-permute-start.10 = (bf16[2,2,16,2048]{3,2,1,0:T(8,128)(2,1)}, bf16[2,2,16,2048]{3,2,1,0:T(8,128)(2,1)S(1)}, u32[]{:S(2)}, u32[]{:S(2)}) collective-permute-start(bf16[2,2,16,2048]{3,2,1,0:T(8,128)(2,1)} %param.4), channel_id=1, source_target_pairs={{22,0},{24,2},{26,4},{28,6},{30,8},{32,10},{34,12},{36,14},{38,16}... | collective-permute-start | bytes 786440 | tf_op jit(solution)/shard_map/ppermute | solution.py:17
  78.8 33.3 %collective-permute-start.11 = (bf16[2,2,16,2048]{3,2,1,0:T(8,128)(2,1)}, bf16[2,2,16,2048]{3,2,1,0:T(8,128)(2,1)S(1)}, u32[]{:S(2)}, u32[]{:S(2)}) collective-permute-start(bf16[2,2,16,2048]{3,2,1,0:T(8,128)(2,1)} %param.4), channel_id=1, source_target_pairs={{24,0},{26,2},{28,4},{30,6},{32,8},{34,10},{36,12},{38,14},{40,16}... | collective-permute-start | bytes 786440 | tf_op jit(solution)/shard_map/ppermute | solution.py:17
  81.7 33.6 %collective-permute-start.12 = (bf16[2,2,16,2048]{3,2,1,0:T(8,128)(2,1)}, bf16[2,2,16,2048]{3,2,1,0:T(8,128)(2,1)S(1)}, u32[]{:S(2)}, u32[]{:S(2)}) collective-permute-start(bf16[2,2,16,2048]{3,2,1,0:T(8,128)(2,1)} %param.4), channel_id=1, source_target_pairs={{26,0},{28,2},{30,4},{32,6},{34,8},{36,10},{38,12},{40,14},{42,16}... | collective-permute-start | bytes 786440 | tf_op jit(solution)/shard_map/ppermute | solution.py:17
  84.6 43.1 %collective-permute-start.13 = (bf16[2,2,16,2048]{3,2,1,0:T(8,128)(2,1)}, bf16[2,2,16,2048]{3,2,1,0:T(8,128)(2,1)S(1)}, u32[]{:S(2)}, u32[]{:S(2)}) collective-permute-start(bf16[2,2,16,2048]{3,2,1,0:T(8,128)(2,1)} %param.4), channel_id=1, source_target_pairs={{28,0},{30,2},{32,4},{34,6},{36,8},{38,10},{40,12},{42,14},{44,16}... | collective-permute-start | bytes 786440 | tf_op jit(solution)/shard_map/ppermute | solution.py:17
  86.1 61.5 %collective-permute-start.14 = (bf16[2,2,16,2048]{3,2,1,0:T(8,128)(2,1)}, bf16[2,2,16,2048]{3,2,1,0:T(8,128)(2,1)}, u32[]{:S(2)}, u32[]{:S(2)}) collective-permute-start(bf16[2,2,16,2048]{3,2,1,0:T(8,128)(2,1)} %param.4), channel_id=1, source_target_pairs={{30,0},{32,2},{34,4},{36,6},{38,8},{40,10},{42,12},{44,14},{46,16}... | collective-permute-start | bytes 786440 | tf_op jit(solution)/shard_map/ppermute | solution.py:17
  110.6 43.5 %collective-permute-start.15 = (bf16[2,2,16,2048]{3,2,1,0:T(8,128)(2,1)}, bf16[2,2,16,2048]{3,2,1,0:T(8,128)(2,1)}, u32[]{:S(2)}, u32[]{:S(2)}) collective-permute-start(bf16[2,2,16,2048]{3,2,1,0:T(8,128)(2,1)} %param.4), channel_id=1, source_target_pairs={{32,0},{34,2},{36,4},{38,6},{40,8},{42,10},{44,12},{46,14},{48,16}... | collective-permute-start | bytes 786440 | tf_op jit(solution)/shard_map/ppermute | solution.py:17
  112.1 48.5 %collective-permute-start.23 = (bf16[2,2,16,2048]{3,2,1,0:T(8,128)(2,1)}, bf16[2,2,16,2048]{3,2,1,0:T(8,128)(2,1)}, u32[]{:S(2)}, u32[]{:S(2)}) collective-permute-start(bf16[2,2,16,2048]{3,2,1,0:T(8,128)(2,1)} %param.4), channel_id=1, source_target_pairs={{48,0},{50,2},{52,4},{54,6},{56,8},{58,10},{60,12},{62,14},{64,16}... | collective-permute-start | bytes 786440 | tf_op jit(solution)/shard_map/ppermute | solution.py:17
  115.3 51.9 %collective-permute-start.16 = (bf16[2,2,16,2048]{3,2,1,0:T(8,128)(2,1)}, bf16[2,2,16,2048]{3,2,1,0:T(8,128)(2,1)}, u32[]{:S(2)}, u32[]{:S(2)}) collective-permute-start(bf16[2,2,16,2048]{3,2,1,0:T(8,128)(2,1)} %param.4), channel_id=1, source_target_pairs={{34,0},{36,2},{38,4},{40,6},{42,8},{44,10},{46,12},{48,14},{50,16}... | collective-permute-start | bytes 786440 | tf_op jit(solution)/shard_map/ppermute | solution.py:17
  127.7 46.1 %collective-permute-start.17 = (bf16[2,2,16,2048]{3,2,1,0:T(8,128)(2,1)}, bf16[2,2,16,2048]{3,2,1,0:T(8,128)(2,1)}, u32[]{:S(2)}, u32[]{:S(2)}) collective-permute-start(bf16[2,2,16,2048]{3,2,1,0:T(8,128)(2,1)} %param.4), channel_id=1, source_target_pairs={{36,0},{38,2},{40,4},{42,6},{44,8},{46,10},{48,12},{50,14},{52,16}... | collective-permute-start | bytes 786440 | tf_op jit(solution)/shard_map/ppermute | solution.py:17
  147.5 32.8 %collective-permute-start.18 = (bf16[2,2,16,2048]{3,2,1,0:T(8,128)(2,1)}, bf16[2,2,16,2048]{3,2,1,0:T(8,128)(2,1)}, u32[]{:S(2)}, u32[]{:S(2)}) collective-permute-start(bf16[2,2,16,2048]{3,2,1,0:T(8,128)(2,1)} %param.4), channel_id=1, source_target_pairs={{38,0},{40,2},{42,4},{44,6},{46,8},{48,10},{50,12},{52,14},{54,16}... | collective-permute-start | bytes 786440 | tf_op jit(solution)/shard_map/ppermute | solution.py:17
  154.1 45.7 %collective-permute-start.19 = (bf16[2,2,16,2048]{3,2,1,0:T(8,128)(2,1)}, bf16[2,2,16,2048]{3,2,1,0:T(8,128)(2,1)}, u32[]{:S(2)}, u32[]{:S(2)}) collective-permute-start(bf16[2,2,16,2048]{3,2,1,0:T(8,128)(2,1)} %param.4), channel_id=1, source_target_pairs={{40,0},{42,2},{44,4},{46,6},{48,8},{50,10},{52,12},{54,14},{56,16}... | collective-permute-start | bytes 786440 | tf_op jit(solution)/shard_map/ppermute | solution.py:17
  160.6 44.4 %collective-permute-start.20 = (bf16[2,2,16,2048]{3,2,1,0:T(8,128)(2,1)}, bf16[2,2,16,2048]{3,2,1,0:T(8,128)(2,1)}, u32[]{:S(2)}, u32[]{:S(2)}) collective-permute-start(bf16[2,2,16,2048]{3,2,1,0:T(8,128)(2,1)} %param.4), channel_id=1, source_target_pairs={{42,0},{44,2},{46,4},{48,6},{50,8},{52,10},{54,12},{56,14},{58,16}... | collective-permute-start | bytes 786440 | tf_op jit(solution)/shard_map/ppermute | solution.py:17
  167.2 66.1 %collective-permute-start.21 = (bf16[2,2,16,2048]{3,2,1,0:T(8,128)(2,1)}, bf16[2,2,16,2048]{3,2,1,0:T(8,128)(2,1)}, u32[]{:S(2)}, u32[]{:S(2)}) collective-permute-start(bf16[2,2,16,2048]{3,2,1,0:T(8,128)(2,1)} %param.4), channel_id=1, source_target_pairs={{44,0},{46,2},{48,4},{50,6},{52,8},{54,10},{56,12},{58,14},{60,16}... | collective-permute-start | bytes 786440 | tf_op jit(solution)/shard_map/ppermute | solution.py:17
  173.7 80.4 %collective-permute-start.22 = (bf16[2,2,16,2048]{3,2,1,0:T(8,128)(2,1)}, bf16[2,2,16,2048]{3,2,1,0:T(8,128)(2,1)}, u32[]{:S(2)}, u32[]{:S(2)}) collective-permute-start(bf16[2,2,16,2048]{3,2,1,0:T(8,128)(2,1)} %param.4), channel_id=1, source_target_pairs={{46,0},{48,2},{50,4},{52,6},{54,8},{56,10},{58,12},{60,14},{62,16}... | collective-permute-start | bytes 786440 | tf_op jit(solution)/shard_map/ppermute | solution.py:17
  180.3 93.9 %collective-permute-start.24 = (bf16[2,2,16,2048]{3,2,1,0:T(8,128)(2,1)}, bf16[2,2,16,2048]{3,2,1,0:T(8,128)(2,1)}, u32[]{:S(2)}, u32[]{:S(2)}) collective-permute-start(bf16[2,2,16,2048]{3,2,1,0:T(8,128)(2,1)} %param.4), channel_id=1, source_target_pairs={{50,0},{52,2},{54,4},{56,6},{58,8},{60,10},{62,12},{64,14},{66,16}... | collective-permute-start | bytes 786440 | tf_op jit(solution)/shard_map/ppermute | solution.py:17
  210.2 11.5 %copy-start.21 = (f32[2,4,4,2048]{3,2,1,0:T(4,128)S(1)}, f32[2,4,4,2048]{3,2,1,0:T(4,128)}, u32[]{:S(2)}) copy-start(f32[2,4,4,2048]{3,2,1,0:T(4,128)} %mul.1995) | copy-start | bytes 786436
  210.2 11.5 %copy-start.22 = (f32[2,4,4,2048]{3,2,1,0:T(4,128)S(1)}, f32[2,4,4,2048]{3,2,1,0:T(4,128)}, u32[]{:S(2)}) copy-start(f32[2,4,4,2048]{3,2,1,0:T(4,128)} %mul.1998) | copy-start | bytes 786436
  210.2 11.5 %copy-start.23 = (f32[2,4,4,2048]{3,2,1,0:T(4,128)S(1)}, f32[2,4,4,2048]{3,2,1,0:T(4,128)}, u32[]{:S(2)}) copy-start(f32[2,4,4,2048]{3,2,1,0:T(4,128)} %mul.2005) | copy-start | bytes 786436
  210.3 11.5 %copy-start.24 = (f32[2,4,4,2048]{3,2,1,0:T(4,128)S(1)}, f32[2,4,4,2048]{3,2,1,0:T(4,128)}, u32[]{:S(2)}) copy-start(f32[2,4,4,2048]{3,2,1,0:T(4,128)} %mul.2008) | copy-start | bytes 786436
  210.3 11.5 %copy-start.25 = (f32[2,4,4,2048]{3,2,1,0:T(4,128)S(1)}, f32[2,4,4,2048]{3,2,1,0:T(4,128)}, u32[]{:S(2)}) copy-start(f32[2,4,4,2048]{3,2,1,0:T(4,128)} %mul.2015) | copy-start | bytes 786436
  210.3 11.5 %copy-start.26 = (f32[2,4,4,2048]{3,2,1,0:T(4,128)S(1)}, f32[2,4,4,2048]{3,2,1,0:T(4,128)}, u32[]{:S(2)}) copy-start(f32[2,4,4,2048]{3,2,1,0:T(4,128)} %mul.2018) | copy-start | bytes 786436
  210.3 11.5 %copy-start.27 = (f32[2,4,4,2048]{3,2,1,0:T(4,128)S(1)}, f32[2,4,4,2048]{3,2,1,0:T(4,128)}, u32[]{:S(2)}) copy-start(f32[2,4,4,2048]{3,2,1,0:T(4,128)} %mul.2025) | copy-start | bytes 786436
  210.3 11.5 %copy-start.28 = (f32[2,4,4,2048]{3,2,1,0:T(4,128)S(1)}, f32[2,4,4,2048]{3,2,1,0:T(4,128)}, u32[]{:S(2)}) copy-start(f32[2,4,4,2048]{3,2,1,0:T(4,128)} %mul.2028) | copy-start | bytes 786436
  210.3 11.5 %copy-start.29 = (f32[2,4,4,2048]{3,2,1,0:T(4,128)S(1)}, f32[2,4,4,2048]{3,2,1,0:T(4,128)}, u32[]{:S(2)}) copy-start(f32[2,4,4,2048]{3,2,1,0:T(4,128)} %mul.2035) | copy-start | bytes 786436
  210.3 11.5 %copy-start.30 = (f32[2,4,4,2048]{3,2,1,0:T(4,128)S(1)}, f32[2,4,4,2048]{3,2,1,0:T(4,128)}, u32[]{:S(2)}) copy-start(f32[2,4,4,2048]{3,2,1,0:T(4,128)} %mul.2038) | copy-start | bytes 786436
  210.3 11.5 %copy-start.31 = (f32[2,4,4,2048]{3,2,1,0:T(4,128)S(1)}, f32[2,4,4,2048]{3,2,1,0:T(4,128)}, u32[]{:S(2)}) copy-start(f32[2,4,4,2048]{3,2,1,0:T(4,128)} %mul.2045) | copy-start | bytes 786436
  210.3 11.5 %copy-start.32 = (f32[2,4,4,2048]{3,2,1,0:T(4,128)S(1)}, f32[2,4,4,2048]{3,2,1,0:T(4,128)}, u32[]{:S(2)}) copy-start(f32[2,4,4,2048]{3,2,1,0:T(4,128)} %mul.2048) | copy-start | bytes 786436
  210.3 11.5 %copy-start.33 = (f32[2,4,4,2048]{3,2,1,0:T(4,128)S(1)}, f32[2,4,4,2048]{3,2,1,0:T(4,128)}, u32[]{:S(2)}) copy-start(f32[2,4,4,2048]{3,2,1,0:T(4,128)} %mul.2055) | copy-start | bytes 786436
  221.8 9.7 %copy-start.34 = (f32[2,4,4,2048]{3,2,1,0:T(4,128)S(1)}, f32[2,4,4,2048]{3,2,1,0:T(4,128)}, u32[]{:S(2)}) copy-start(f32[2,4,4,2048]{3,2,1,0:T(4,128)} %mul.2058) | copy-start | bytes 786436
  221.8 10.6 %copy-start.35 = (f32[2,4,4,2048]{3,2,1,0:T(4,128)S(1)}, f32[2,4,4,2048]{3,2,1,0:T(4,128)}, u32[]{:S(2)}) copy-start(f32[2,4,4,2048]{3,2,1,0:T(4,128)} %mul.2065) | copy-start | bytes 786436
  221.9 10.6 %copy-start.36 = (f32[2,4,4,2048]{3,2,1,0:T(4,128)S(1)}, f32[2,4,4,2048]{3,2,1,0:T(4,128)}, u32[]{:S(2)}) copy-start(f32[2,4,4,2048]{3,2,1,0:T(4,128)} %mul.2068) | copy-start | bytes 786436
  252.4 9.6 %copy-start.11 = (f32[2,4,4,2048]{3,2,1,0:T(4,128)S(1)}, f32[2,4,4,2048]{3,2,1,0:T(4,128)}, u32[]{:S(2)}) copy-start(f32[2,4,4,2048]{3,2,1,0:T(4,128)} %mul.2175) | copy-start | bytes 786436
  252.4 9.6 %copy-start.12 = (f32[2,4,4,2048]{3,2,1,0:T(4,128)S(1)}, f32[2,4,4,2048]{3,2,1,0:T(4,128)}, u32[]{:S(2)}) copy-start(f32[2,4,4,2048]{3,2,1,0:T(4,128)} %mul.2178) | copy-start | bytes 786436
  252.4 10.4 %copy-start.13 = (f32[2,4,4,2048]{3,2,1,0:T(4,128)S(1)}, f32[2,4,4,2048]{3,2,1,0:T(4,128)}, u32[]{:S(2)}) copy-start(f32[2,4,4,2048]{3,2,1,0:T(4,128)} %mul.2185) | copy-start | bytes 786436
  252.4 10.4 %copy-start.14 = (f32[2,4,4,2048]{3,2,1,0:T(4,128)S(1)}, f32[2,4,4,2048]{3,2,1,0:T(4,128)}, u32[]{:S(2)}) copy-start(f32[2,4,4,2048]{3,2,1,0:T(4,128)} %mul.2188) | copy-start | bytes 786436
  252.4 11.2 %copy-start.15 = (f32[2,4,4,2048]{3,2,1,0:T(4,128)S(1)}, f32[2,4,4,2048]{3,2,1,0:T(4,128)}, u32[]{:S(2)}) copy-start(f32[2,4,4,2048]{3,2,1,0:T(4,128)} %mul.2195) | copy-start | bytes 786436
  353.6 48.8 %copy-start.37 = (s32[256,24]{0,1:T(8,128)S(1)}, s32[256,24]{0,1:T(8,128)}, u32[]{:S(2)}) copy-start(s32[256,24]{0,1:T(8,128)} %param.5) | copy-start | bytes 73732
  362.1 54.3 %all-to-all-start.1 = ((f32[2,2,128,96]{3,1,0,2:T(2,128)}), f32[2,2,128,96]{3,1,0,2:T(2,128)S(1)}, u32[]{:S(2)}, u32[]{:S(2)}) async-start(f32[2,2,128,96]{3,1,0,2:T(2,128)} %copy.426), calls=%async_computation.1 | async-start | bytes 524288 | tf_op jit(solution)/shard_map/all_to_all | solution.py:121
  (138 other events, 671.9 us)
where the time goes:
time: 539 us; the launch traced here: 529 us
  matrix products  167 us (31%)
  local copies, waits for them, and re-layouts  127 us (24%)
  starting transfers between devices  85.3 us (16%)
  waiting for transfers between devices  73.8 us (14%)
  other arithmetic  66.6 us (12%)
    dot_general x78, matrix products, box_mean(): return jnp.matmul(row_sums, boxcar, precision=highest) / 64.0  69.7 us
    ppermute x25, waiting for transfers between devices, passed_along(): return lax.ppermute(value, axis, pairs)  60 us
    reduce_sum x30, other arithmetic, box_mean(): jnp.sum(values.reshape(layout[:-2] + (layout[-2] // 4, 4, layout[-1])), a...  54.1 us
    ppermute x25, starting transfers between devices, passed_along(): return lax.ppermute(value, axis, pairs)  45 us
    all_to_all x1, starting transfers between devices, on_device(): lax.all_to_all(on_cores, 'date', split_axis=2, concat_axis=1, tiled=True)  40.3 us
    broadcast_in_dim x182, local copies, waits for them, and re-layouts, absorb(): jnp.where(chosen, pair_real[:, member][:, None], 0.0)  37.9 us
    mul x26, local copies, waits for them, and re-layouts, absorb(): own_float[1][:, None] * tile_float[1][None]  27.7 us
    mul x26, local copies, waits for them, and re-layouts, absorb(): own_float[0][:, None] * tile_float[0][None]  26.1 us
  transfers between devices with their start and end apart: 26, of which 6 were waited for; matrix products, arithmetic and copies ran while one was open for 32% of the time, Pallas kernels for 0%

commit v1 on v0

v1 whole, which is shorter than its diff:
```python
import functools

import jax
import jax.numpy as jnp
from jax import lax
from jax.experimental import pallas as pl
from jax.experimental.pallas import tpu as pltpu
from jax.sharding import PartitionSpec as P

EPSILON = 1e-06
BLOCKS = 5
MESH = pl.DeviceIdType.MESH


def halves(value):
    high = value.astype(jnp.bfloat16)
    low = (value - high.astype(jnp.float32)).astype(jnp.bfloat16)
    return high, low


def product(left, right):
    return jnp.dot(left, right, preferred_element_type=jnp.float32)


def gram(left, right):
    return lax.dot_general(left, right, (((1,), (1,)), ((), ())), preferred_element_type=jnp.float32)


def squared(real, imag):
    real_high, real_low = real
    imag_high, imag_low = imag
    cross = product(real_high, real_low) - product(imag_high, imag_low)
    out_real = product(real_high, real_high) - product(imag_high, imag_high) + (cross + cross.T)
    mixed = product(real_high, imag_high) + product(real_high, imag_low) + product(real_low, imag_high)
    return out_real, mixed - mixed.T


def applied(real, imag, rows):
    count = rows.shape[0]
    high, low = halves(rows)
    stacked = jnp.concatenate([high, low], axis=0)
    by_real = product(stacked, real[0])
    by_imag = product(stacked, imag[0])
    by_real = by_real[:count] + by_real[count:] + product(high, real[1])
    by_imag = by_imag[:count] + by_imag[count:] + product(high, imag[1])
    half = count // 2
    return jnp.concatenate([by_real[:half] + by_imag[half:], by_real[half:] - by_imag[:half]], axis=0)


def power_mean(rows):
    half = rows.shape[0] // 2
    squares = rows[:half] * rows[:half] + rows[half:] * rows[half:]
    return jnp.mean(squares, axis=1, keepdims=True)


def linked_phase(images, pairs):
    dates = images.shape[0]
    turned = jnp.concatenate([images[:, 64:], -images[:, :64]], axis=1)
    cov_real = gram(images, images) * (1.0 / 64.0)
    cov_imag = gram(turned, images) * (1.0 / 64.0)
    row = lax.broadcasted_iota(jnp.int32, (dates, dates), 0)
    col = lax.broadcasted_iota(jnp.int32, (dates, dates), 1)
    diagonal = row == col
    only = jnp.where(diagonal, cov_real, 0.0)
    scale_row = lax.rsqrt(jnp.sum(only, axis=0, keepdims=True) + EPSILON)
    scale_col = lax.rsqrt(jnp.sum(only, axis=1, keepdims=True) + EPSILON)
    weight = pairs * scale_row * scale_col
    herm_real = jnp.where(diagonal, 1.0, cov_real * weight)
    herm_imag = cov_imag * weight
    first = halves(herm_real), halves(herm_imag)
    square = squared(*first)
    second = halves(square[0]), halves(square[1])
    fourth = squared(*second)
    fourth = halves(fourth[0]), halves(fourth[1])

    ones = jnp.ones((1, dates), jnp.float32)
    none = jnp.zeros((1, dates), jnp.float32)
    pad = jnp.zeros((6, dates), jnp.float32)
    start = jnp.concatenate([ones, none, pad], axis=0)
    start = jnp.concatenate([ones, jnp.zeros((7, dates), jnp.float32)], axis=0)
    one = applied(*first, start)
    pair = jnp.concatenate([ones, one[0:1], none, none, none, one[4:5], none, none], axis=0)
    later = applied(*second, pair)
    rows = jnp.concatenate([ones, one[0:1], later[0:2], none, one[4:5], later[4:6]], axis=0)
    for _ in range(BLOCKS):
        after = applied(*fourth, rows)
        means = power_mean(rows)
        ratio = 1.0
        for step in (1, 2, 3):
            ratio = ratio * lax.rsqrt(ratio * ratio * means[step : step + 1] + EPSILON)
        ratio = ratio * lax.rsqrt(ratio * ratio * power_mean(after)[0:1] + EPSILON)
        rows = after * ratio
    return rows[0:1], rows[4:5]


def pair_mask(offsets):
    dates, slots = offsets.shape
    row = lax.broadcasted_iota(jnp.int32, (dates, dates), 0)
    col = lax.broadcasted_iota(jnp.int32, (dates, dates), 1)
    apart = jnp.where(col > row, col - row, -1)
    upper = jnp.zeros((dates, dates), jnp.float32)
    for slot in range(slots):
        upper = jnp.where(offsets[:, slot : slot + 1] == apart, 1.0, upper)
    return upper + upper.T


def kernel(
    groups,
    slc_ref,
    offsets_ref,
    out_ref,
    strip,
    table,
    wide,
    outgoing,
    arrived,
    ordered,
    strip_sem,
    table_sem,
    send_sem,
    recv_sem,
):
    date = lax.axis_index("date")
    core = lax.axis_index("col")
    chunks = outgoing.shape[0]
    owners = chunks // 2
    side = date // owners
    own = side == core

    barrier = pltpu.get_barrier_semaphore()

    def greet(step, carry):
        source = lax.rem(date + step, groups)

        @pl.when(jnp.logical_not((step == 0) & own))
        def _():
            pl.semaphore_signal(barrier, inc=1, device_id=(source, side), device_id_type=MESH)

        return carry

    load_strip = pltpu.make_async_copy(slc_ref, strip, strip_sem)
    load_strip.start()
    load_table = pltpu.make_async_copy(offsets_ref, table, table_sem)
    load_table.start()
    lax.fori_loop(0, groups, greet, 0)

    load_strip.wait()
    lane = lax.broadcasted_iota(jnp.int32, (8, 128), 1)

    def regroup(tile, carry):
        columns = pl.ds(pl.multiple_of(tile * 128, 128), 128)
        for part in range(2):
            for t in range(2):
                wide[tile, pl.ds(part * 32 + t * 16, 16), :] = strip[part, t, :, columns].astype(jnp.float32)
        group = [wide[tile, pl.ds((g // 4) * 32 + g % 4, 8, stride=4), :] for g in range(8)]
        for bit in range(3):
            shift = 16 << bit
            upper = (lane & shift) != 0
            for g in range(8):
                other = g | (1 << bit)
                if other != g:
                    low, high = group[g], group[other]
                    group[g] = jnp.where(upper, pltpu.roll(high, shift, 1), low)
                    group[other] = jnp.where(upper, high, pltpu.roll(low, 128 - shift, 1))
        for g in range(8):
            outgoing[tile * 8 + g] = group[g].astype(jnp.bfloat16)
        return carry

    lax.fori_loop(0, chunks // 8, regroup, 0)

    pl.semaphore_wait(barrier, jnp.where(own, chunks - 1, chunks))

    def send(step, carry):
        chunk = lax.rem(2 * date + step, chunks)
        owner = owners * core + chunk // 2
        owner_core = lax.rem(chunk, 2)
        stays = (owner == date) & (owner_core == core)

        @pl.when(jnp.logical_not(stays))
        def _():
            pltpu.make_async_remote_copy(
                src_ref=outgoing.at[chunk],
                dst_ref=arrived.at[date],
                send_sem=send_sem,
                recv_sem=recv_sem,
                device_id=(owner, owner_core),
                device_id_type=MESH,
            ).start()

        @pl.when(stays)
        def _():
            pltpu.make_async_copy(outgoing.at[chunk], arrived.at[date], recv_sem).start()

        return carry

    lax.fori_loop(0, chunks, send, 0)

    load_table.wait()
    pairs = pair_mask(table[...])

    pltpu.make_async_copy(arrived, arrived, recv_sem).wait()
    wide_rows = arrived[...].astype(jnp.float32).reshape(groups * 8, 128)
    ordered[0 : groups * 8, :] = wide_rows
    for pixel in range(4):
        for t in range(2):
            picked = ordered[pl.ds(t * 4 + pixel, groups, stride=8), :]
            ordered[pl.ds(groups * 8 + pixel * 2 * groups + t, groups, stride=2), :] = picked
    for pixel in range(4):
        first = groups * 8 + pixel * 2 * groups
        images = ordered[first : first + 2 * groups, :].astype(jnp.bfloat16)
        real, imag = linked_phase(images, pairs)
        out_ref[0, pixel] = real
        out_ref[1, pixel] = imag

    @pl.when(own)
    def _():
        rest = outgoing.at[pl.ds(0, chunks - 1)]
        pltpu.make_async_copy(rest, rest, send_sem).wait()

    @pl.when(jnp.logical_not(own))
    def _():
        pltpu.make_async_copy(outgoing, outgoing, send_sem).wait()


def solution(mesh):
    groups = mesh.shape["date"]

    def on_device(slc, partner_offsets):
        dates = slc.shape[1] * groups
        chunks = slc.shape[3] // 16
        return pl.pallas_call(
            functools.partial(kernel, groups),
            out_shape=jax.ShapeDtypeStruct((2, 4, 1, dates), jnp.float32),
            in_specs=[pl.BlockSpec(memory_space=pl.ANY)] * 2,
            out_specs=pl.BlockSpec(memory_space=pltpu.VMEM),
            scratch_shapes=[
                pltpu.VMEM(slc.shape, jnp.bfloat16),
                pltpu.VMEM(partner_offsets.shape, jnp.int32),
                pltpu.VMEM((chunks // 8, 64, 128), jnp.float32),
                pltpu.VMEM((chunks, 8, 128), jnp.bfloat16),
                pltpu.VMEM((groups, 8, 128), jnp.bfloat16),
                pltpu.VMEM((groups * 8 + 4 * dates, 128), jnp.float32),
                pltpu.SemaphoreType.DMA,
                pltpu.SemaphoreType.DMA,
                pltpu.SemaphoreType.DMA,
                pltpu.SemaphoreType.DMA,
            ],
            compiler_params=pltpu.CompilerParams(
                collective_id=0, has_side_effects=True, vmem_limit_bytes=48 * 1024 * 1024
            ),
        )(slc, partner_offsets)

    return jax.shard_map(
        on_device,
        mesh=mesh,
        in_specs=(P(None, "date", None, "col"), P()),
        out_specs=P(None, None, ("date", "col"), None),
        check_vma=False,
    )
```

time: 539 us -> 38.5 us (0.07); the launches traced: 529 us -> 38.3 us
  matrix products: 167 us -> 0 us
  local copies, waits for them, and re-layouts: 127 us -> 2.38 us
  starting transfers between devices: 85.3 us -> 0 us
  waiting for transfers between devices: 73.8 us -> 0 us
  other arithmetic: 66.6 us -> 0 us
  Pallas kernels: 0 us -> 35.9 us
    dot_general x160 -> x0, matrix products: 167 us -> none  [the longest x78 69.7 us: box_mean(): return jnp.matmul(row_sums, boxcar, precision=highest) / 64.0]
    ppermute x25 -> x0, waiting for transfers between devices: 60 us -> none  [passed_along(): return lax.ppermute(value, axis, pairs)]
    reduce_sum x50 -> x0, other arithmetic: 56.8 us -> none  [the longest x30 54.1 us: box_mean(): jnp.sum(values.reshape(layout[:-2] + (layout[-2] // 4, 4, layout[-1])), a...]
    mul x52 -> x0, local copies, waits for them, and re-layouts: 53.7 us -> none  [the longest x26 27.7 us: absorb(): own_float[1][:, None] * tile_float[1][None]]
    ppermute x25 -> x0, starting transfers between devices: 45 us -> none  [passed_along(): return lax.ppermute(value, axis, pairs)]
    all_to_all x1 -> x0, starting transfers between devices: 40.3 us -> none  [on_device(): lax.all_to_all(on_cores, 'date', split_axis=2, concat_axis=1, tiled=True)]
    broadcast_in_dim x260 -> x0, local copies, waits for them, and re-layouts: 38.7 us -> none  [the longest x182 37.9 us: absorb(): jnp.where(chosen, pair_real[:, member][:, None], 0.0)]
    pallas_call x0 -> x1, Pallas kernels: none -> 35.9 us  [on_device(): pl.pallas_call(functools.partial(kernel, groups), out_shape=jax.ShapeDtyp...]
  transfers between devices with their start and end apart: 26 -> 0, of which waited for: 6 -> 0; matrix products, arithmetic and copies ran while one was open for 32% -> 0% of each run, Pallas kernels for 0% -> 0%
where the time goes in v1:
time: 38.5 us; the launch traced here: 38.3 us
  Pallas kernels  35.9 us (93%)
  local copies, waits for them, and re-layouts  2.38 us (6%)
    pallas_call x1, Pallas kernels, on_device(): pl.pallas_call(functools.partial(kernel, groups), out_shape=jax.ShapeDtyp...  35.9 us
    unnamed x4, local copies, waits for them, and re-layouts  2.38 us

profile of v1, /device:TPU:1, one launch (start us, length us, event | category | flops | bytes accessed | tf_op | source)
XLA Modules:
  0.0 38.3 jit_solution(7426555559261144519)
XLA Ops:
  0.0 0.8 %copy.3.offsets_ref = s32[256,24]{1,0:T(8,128)S(1)} copy(s32[256,24]{0,1:T(8,128)} %param.3) | data formatting | bytes 49152 | tf_op args[1]
  0.8 0.0 copy-start
  0.8 0.9 %copy-done = bf16[2,2,16,2048]{3,2,1,0:T(8,128)(2,1)S(1)} copy-done((bf16[2,2,16,2048]{3,2,1,0:T(8,128)(2,1)S(1)}, bf16[2,2,16,2048]{3,2,1,0:T(8,128)(2,1)}, u32[]{:S(2)}) %copy-start) | copy-done | bytes 262168
  1.8 35.9 %shard_map.28 = f32[2,4,1,256]{3,2,1,0:T(1,128)S(1)} custom-call(bf16[2,2,16,2048]{3,2,1,0:T(8,128)(2,1)S(1)} %copy-done, s32[256,24]{1,0:T(8,128)S(1)} %copy.3.offsets_ref), custom_call_target="tpu_custom_call" | custom-call | tf_op jit(solution)/shard_map/pallas_call | solution.py:231
  37.7 0.6 %copy.5 = f32[2,4,1,256]{3,2,1,0:T(1,128)} copy(f32[2,4,1,256]{3,2,1,0:T(1,128)S(1)} %shard_map.28) | data formatting | bytes 16384
Async XLA Ops:
  0.8 1.0 %copy-start = (bf16[2,2,16,2048]{3,2,1,0:T(8,128)(2,1)S(1)}, bf16[2,2,16,2048]{3,2,1,0:T(8,128)(2,1)}, u32[]{:S(2)}) copy-start(bf16[2,2,16,2048]{3,2,1,0:T(8,128)(2,1)} %slc_ref.1) | copy-start | bytes 786436

commit v2 on v1

--- a/solution.py
+++ b/solution.py
@@ -8,7 +8,8 @@
 from jax.sharding import PartitionSpec as P
 
 EPSILON = 1e-06
-BLOCKS = 5
+STRIDES = 4
+VMEM_BYTES = 56_545_280
 MESH = pl.DeviceIdType.MESH
 
 
@@ -27,8 +28,8 @@
 
 
 def squared(real, imag):
-    real_high, real_low = real
-    imag_high, imag_low = imag
+    real_high, real_low = halves(real)
+    imag_high, imag_low = halves(imag)
     cross = product(real_high, real_low) - product(imag_high, imag_low)
     out_real = product(real_high, real_high) - product(imag_high, imag_high) + (cross + cross.T)
     mixed = product(real_high, imag_high) + product(real_high, imag_low) + product(real_low, imag_high)
@@ -37,71 +38,78 @@
 
 def applied(real, imag, rows):
     count = rows.shape[0]
+    half = count // 2
     high, low = halves(rows)
     stacked = jnp.concatenate([high, low], axis=0)
     by_real = product(stacked, real[0])
     by_imag = product(stacked, imag[0])
     by_real = by_real[:count] + by_real[count:] + product(high, real[1])
     by_imag = by_imag[:count] + by_imag[count:] + product(high, imag[1])
-    half = count // 2
     return jnp.concatenate([by_real[:half] + by_imag[half:], by_real[half:] - by_imag[:half]], axis=0)
 
 
-def power_mean(rows):
-    half = rows.shape[0] // 2
-    squares = rows[:half] * rows[:half] + rows[half:] * rows[half:]
-    return jnp.mean(squares, axis=1, keepdims=True)
-
-
-def linked_phase(images, pairs):
-    dates = images.shape[0]
+def coherences(images, pairs, diagonal):
     turned = jnp.concatenate([images[:, 64:], -images[:, :64]], axis=1)
     cov_real = gram(images, images) * (1.0 / 64.0)
     cov_imag = gram(turned, images) * (1.0 / 64.0)
-    row = lax.broadcasted_iota(jnp.int32, (dates, dates), 0)
-    col = lax.broadcasted_iota(jnp.int32, (dates, dates), 1)
-    diagonal = row == col
     only = jnp.where(diagonal, cov_real, 0.0)
     scale_row = lax.rsqrt(jnp.sum(only, axis=0, keepdims=True) + EPSILON)
     scale_col = lax.rsqrt(jnp.sum(only, axis=1, keepdims=True) + EPSILON)
     weight = pairs * scale_row * scale_col
-    herm_real = jnp.where(diagonal, 1.0, cov_real * weight)
-    herm_imag = cov_imag * weight
-    first = halves(herm_real), halves(herm_imag)
-    square = squared(*first)
-    second = halves(square[0]), halves(square[1])
-    fourth = squared(*second)
-    fourth = halves(fourth[0]), halves(fourth[1])
-
-    ones = jnp.ones((1, dates), jnp.float32)
-    none = jnp.zeros((1, dates), jnp.float32)
-    pad = jnp.zeros((6, dates), jnp.float32)
-    start = jnp.concatenate([ones, none, pad], axis=0)
-    start = jnp.concatenate([ones, jnp.zeros((7, dates), jnp.float32)], axis=0)
-    one = applied(*first, start)
-    pair = jnp.concatenate([ones, one[0:1], none, none, none, one[4:5], none, none], axis=0)
-    later = applied(*second, pair)
-    rows = jnp.concatenate([ones, one[0:1], later[0:2], none, one[4:5], later[4:6]], axis=0)
-    for _ in range(BLOCKS):
-        after = applied(*fourth, rows)
-        means = power_mean(rows)
-        ratio = 1.0
-        for step in (1, 2, 3):
-            ratio = ratio * lax.rsqrt(ratio * ratio * means[step : step + 1] + EPSILON)
-        ratio = ratio * lax.rsqrt(ratio * ratio * power_mean(after)[0:1] + EPSILON)
-        rows = after * ratio
-    return rows[0:1], rows[4:5]
-
-
-def pair_mask(offsets):
-    dates, slots = offsets.shape
+    return jnp.where(diagonal, 1.0, cov_real * weight), cov_imag * weight
+
+
+def times_ones(real, imag):
+    return jnp.sum(real, axis=0, keepdims=True), -jnp.sum(imag, axis=0, keepdims=True)
+
+
+def mean_product(a, b):
+    return jnp.mean(a[0] * b[0] + a[1] * b[1], axis=1, keepdims=True)
+
+
+def folded(tail, means):
+    for mean in means:
+        tail = mean + EPSILON * tail
+    return tail
+
+
+def linked_phases(images, pairs):
+    dates = pairs.shape[0]
     row = lax.broadcasted_iota(jnp.int32, (dates, dates), 0)
     col = lax.broadcasted_iota(jnp.int32, (dates, dates), 1)
-    apart = jnp.where(col > row, col - row, -1)
-    upper = jnp.zeros((dates, dates), jnp.float32)
+    first = [coherences(image, pairs, row == col) for image in images]
+    second = [squared(*matrix) for matrix in first]
+    two = [times_ones(*matrix) for matrix in second]
+    fourth = [squared(*matrix) for matrix in second]
+    four = [times_ones(*matrix) for matrix in fourth]
+    fourth = [(halves(real), halves(imag)) for real, imag in fourth]
+    ones = jnp.ones((1, dates), jnp.float32), jnp.zeros((1, dates), jnp.float32)
+    pad = jnp.zeros((2, dates), jnp.float32)
+    rows = []
+    for a, b in zip(two, four):
+        means = [mean_product(ones, a), mean_product(a, a), mean_product(a, b), mean_product(b, b)]
+        value = jnp.concatenate([b[0], a[0], pad, b[1], a[1], pad], axis=0)
+        rows.append(value * lax.rsqrt(folded(1.0, means)))
+    for _ in range(STRIDES):
+        after = [applied(*matrix, value) for matrix, value in zip(fourth, rows)]
+        for pixel in range(len(rows)):
+            old, new = rows[pixel], after[pixel]
+            k = old[0:1], old[4:5]
+            a, b = (new[1:2], new[5:6]), (new[0:1], new[4:5])
+            means = [mean_product(k, a), mean_product(a, a), mean_product(a, b), mean_product(b, b)]
+            rows[pixel] = new * lax.rsqrt(folded(1.0, means))
+    return [(value[0:1], value[4:5]) for value in rows]
+
+
+def pair_mask(offsets):
+    slots, dates = offsets.shape
+    row = lax.broadcasted_iota(jnp.int32, (dates, dates), 0)
+    col = lax.broadcasted_iota(jnp.int32, (dates, dates), 1)
+    apart = jnp.where(row > col, row - col, -1)
+    lower = jnp.zeros((dates, dates), jnp.float32)
     for slot in range(slots):
-        upper = jnp.where(offsets[:, slot : slot + 1] == apart, 1.0, upper)
-    return upper + upper.T
+        lower = jnp.where(offsets[slot : slot + 1, :] == apart, 1.0, lower)
+    return lower + lower.T
 
 
 def kernel(
@@ -205,10 +213,11 @@
         for t in range(2):
             picked = ordered[pl.ds(t * 4 + pixel, groups, stride=8), :]
             ordered[pl.ds(groups * 8 + pixel * 2 * groups + t, groups, stride=2), :] = picked
+    images = []
     for pixel in range(4):
         first = groups * 8 + pixel * 2 * groups
-        images = ordered[first : first + 2 * groups, :].astype(jnp.bfloat16)
-        real, imag = linked_phase(images, pairs)
+        images.append(ordered[first : first + 2 * groups, :].astype(jnp.bfloat16))
+    for pixel, (real, imag) in enumerate(linked_phases(images, pairs)):
         out_ref[0, pixel] = real
         out_ref[1, pixel] = imag
 
@@ -231,11 +240,11 @@
         return pl.pallas_call(
             functools.partial(kernel, groups),
             out_shape=jax.ShapeDtypeStruct((2, 4, 1, dates), jnp.float32),
-            in_specs=[pl.BlockSpec(memory_space=pl.ANY)] * 2,
+            in_specs=[pl.BlockSpec(memory_space=pltpu.HBM)] * 2,
             out_specs=pl.BlockSpec(memory_space=pltpu.VMEM),
             scratch_shapes=[
                 pltpu.VMEM(slc.shape, jnp.bfloat16),
-                pltpu.VMEM(partner_offsets.shape, jnp.int32),
+                pltpu.VMEM(partner_offsets.shape[::-1], jnp.int32),
                 pltpu.VMEM((chunks // 8, 64, 128), jnp.float32),
                 pltpu.VMEM((chunks, 8, 128), jnp.bfloat16),
                 pltpu.VMEM((groups, 8, 128), jnp.bfloat16),
@@ -246,9 +255,9 @@
                 pltpu.SemaphoreType.DMA,
             ],
             compiler_params=pltpu.CompilerParams(
-                collective_id=0, has_side_effects=True, vmem_limit_bytes=48 * 1024 * 1024
+                collective_id=0, has_side_effects=True, vmem_limit_bytes=VMEM_BYTES
             ),
-        )(slc, partner_offsets)
+        )(slc, partner_offsets.T)
 
     return jax.shard_map(
         on_device,

time: 38.5 us -> 29.3 us (0.76)
  Pallas kernels: 35.9 us -> 28.6 us
  local copies, waits for them, and re-layouts: 2.38 us -> 0.6 us
    pallas_call x1, Pallas kernels: 35.9 us -> 28.6 us  [on_device(): pl.pallas_call(functools.partial(kernel, groups), out_shape=jax.ShapeDtyp...]
    unnamed x4 -> x1, local copies, waits for them, and re-layouts: 2.38 us -> 0.6 us
where the time goes in v2:
time: 29.3 us; the launch traced here: 29.2 us
  Pallas kernels  28.6 us (98%)
  local copies, waits for them, and re-layouts  0.6 us (2%)
    pallas_call x1, Pallas kernels, on_device(): pl.pallas_call(functools.partial(kernel, groups), out_shape=jax.ShapeDtyp...  28.6 us
    unnamed x1, local copies, waits for them, and re-layouts  0.6 us

profile of v2, /device:TPU:1, one launch (start us, length us, event | category | flops | bytes accessed | tf_op | source)
XLA Modules:
  0.0 29.2 jit_solution(792930497606607649)
XLA Ops:
  0.0 28.6 %shard_map.28 = f32[2,4,1,256]{3,2,1,0:T(1,128)S(1)} custom-call(bf16[2,2,16,2048]{3,2,1,0:T(8,128)(2,1)} %slc_ref.1, s32[24,256]{1,0:T(8,128)} %bitcast.1), custom_call_target="tpu_custom_call" | custom-call | tf_op jit(solution)/shard_map/pallas_call | solution.py:240
  28.6 0.6 %copy.4 = f32[2,4,1,256]{3,2,1,0:T(1,128)} copy(f32[2,4,1,256]{3,2,1,0:T(1,128)S(1)} %shard_map.28) | data formatting | bytes 16384

commit v3 on v2

--- a/solution.py
+++ b/solution.py
@@ -10,6 +10,7 @@
 EPSILON = 1e-06
 STRIDES = 4
 VMEM_BYTES = 56_545_280
+DEPTH = 8
 MESH = pl.DeviceIdType.MESH
 
 
@@ -139,18 +140,19 @@
 
     def greet(step, carry):
         source = lax.rem(date + step, groups)
-
-        @pl.when(jnp.logical_not((step == 0) & own))
-        def _():
-            pl.semaphore_signal(barrier, inc=1, device_id=(source, side), device_id_type=MESH)
-
+        pl.semaphore_signal(barrier, inc=1, device_id=(source, side), device_id_type=MESH)
         return carry
 
     load_strip = pltpu.make_async_copy(slc_ref, strip, strip_sem)
     load_strip.start()
     load_table = pltpu.make_async_copy(offsets_ref, table, table_sem)
     load_table.start()
-    lax.fori_loop(0, groups, greet, 0)
+    lax.fori_loop(1, groups, greet, 0)
+
+    @pl.when(jnp.logical_not(own))
+    def _():
+        greet(0, 0)
+
 
     load_strip.wait()
     lane = lax.broadcasted_iota(jnp.int32, (8, 128), 1)
@@ -174,12 +176,13 @@
             outgoing[tile * 8 + g] = group[g].astype(jnp.bfloat16)
         return carry
 
-    lax.fori_loop(0, chunks // 8, regroup, 0)
+    lax.fori_loop(0, chunks // 8, regroup, 0, unroll=8)
 
     pl.semaphore_wait(barrier, jnp.where(own, chunks - 1, chunks))
 
     def send(step, carry):
-        chunk = lax.rem(2 * date + step, chunks)
+        y, z, x = lax.rem(step // 2, 4), lax.rem(step // 8, DEPTH), step // (8 * DEPTH)
+        chunk = ((x * 4 + y) * DEPTH + z) * 2 + lax.rem(step, 2)
         owner = owners * core + chunk // 2
         owner_core = lax.rem(chunk, 2)
         stays = (owner == date) & (owner_core == core)

time: 29.3 us -> 25.4 us (0.87)
  the two profiles are of different devices: /device:TPU:1 before, /device:TPU:3 now
where the time goes in v3:
time: 25.4 us; the launch traced here: 25.3 us
  Pallas kernels  24.7 us (97%)
  local copies, waits for them, and re-layouts  0.6 us (2%)
    pallas_call x1, Pallas kernels, on_device(): pl.pallas_call(functools.partial(kernel, groups), out_shape=jax.ShapeDtyp...  24.7 us
    unnamed x1, local copies, waits for them, and re-layouts  0.6 us

profile of v3, /device:TPU:3, one launch (start us, length us, event | category | flops | bytes accessed | tf_op | source)
XLA Modules:
  0.0 25.3 jit_solution(6676848288219919388)
XLA Ops:
  0.0 24.7 %shard_map.28 = f32[2,4,1,256]{3,2,1,0:T(1,128)S(1)} custom-call(bf16[2,2,16,2048]{3,2,1,0:T(8,128)(2,1)} %slc_ref.1, s32[24,256]{1,0:T(8,128)} %bitcast.1), custom_call_target="tpu_custom_call" | custom-call | tf_op jit(solution)/shard_map/pallas_call | solution.py:243
  24.7 0.6 %copy.4 = f32[2,4,1,256]{3,2,1,0:T(1,128)} copy(f32[2,4,1,256]{3,2,1,0:T(1,128)S(1)} %shard_map.28) | data formatting | bytes 16384

commit v4 on v3

--- a/solution.py
+++ b/solution.py
@@ -11,6 +11,7 @@
 STRIDES = 4
 VMEM_BYTES = 56_545_280
 DEPTH = 8
+NEAR = 3
 MESH = pl.DeviceIdType.MESH
 
 
@@ -31,10 +32,11 @@
 def squared(real, imag):
     real_high, real_low = halves(real)
     imag_high, imag_low = halves(imag)
-    cross = product(real_high, real_low) - product(imag_high, imag_low)
-    out_real = product(real_high, real_high) - product(imag_high, imag_high) + (cross + cross.T)
+    sum_high = (real + imag).astype(jnp.bfloat16)
+    less_high, less_low = halves(real - imag)
     mixed = product(real_high, imag_high) + product(real_high, imag_low) + product(real_low, imag_high)
-    return out_real, mixed - mixed.T
+    part = product(sum_high, less_low) + mixed
+    return product(sum_high, less_high) + (part + part.T), mixed - mixed.T
 
 
 def applied(real, imag, rows):
@@ -86,19 +88,21 @@
     fourth = [(halves(real), halves(imag)) for real, imag in fourth]
     ones = jnp.ones((1, dates), jnp.float32), jnp.zeros((1, dates), jnp.float32)
     pad = jnp.zeros((2, dates), jnp.float32)
-    rows = []
+    rows, tails = [], []
     for a, b in zip(two, four):
         means = [mean_product(ones, a), mean_product(a, a), mean_product(a, b), mean_product(b, b)]
-        value = jnp.concatenate([b[0], a[0], pad, b[1], a[1], pad], axis=0)
-        rows.append(value * lax.rsqrt(folded(1.0, means)))
+        rows.append(jnp.concatenate([b[0], a[0], pad, b[1], a[1], pad], axis=0))
+        tails.append(folded(1.0, means))
     for _ in range(STRIDES):
         after = [applied(*matrix, value) for matrix, value in zip(fourth, rows)]
         for pixel in range(len(rows)):
-            old, new = rows[pixel], after[pixel]
-            k = old[0:1], old[4:5]
-            a, b = (new[1:2], new[5:6]), (new[0:1], new[4:5])
+            old, new, scale = rows[pixel], after[pixel], lax.rsqrt(tails[pixel])
+            rows[pixel] = new * scale
+            k = old[0:1] * scale, old[4:5] * scale
+            a, b = (rows[pixel][1:2], rows[pixel][5:6]), (rows[pixel][0:1], rows[pixel][4:5])
             means = [mean_product(k, a), mean_product(a, a), mean_product(a, b), mean_product(b, b)]
-            rows[pixel] = new * lax.rsqrt(folded(1.0, means))
+            tails[pixel] = folded(1.0, means)
+    rows = [value * lax.rsqrt(tail) for value, tail in zip(rows, tails)]
     return [(value[0:1], value[4:5]) for value in rows]
 
 
@@ -128,6 +132,7 @@
     table_sem,
     send_sem,
     recv_sem,
+    other,
 ):
     date = lax.axis_index("date")
     core = lax.axis_index("col")
@@ -138,21 +143,31 @@
 
     barrier = pltpu.get_barrier_semaphore()
 
-    def greet(step, carry):
-        source = lax.rem(date + step, groups)
-        pl.semaphore_signal(barrier, inc=1, device_id=(source, side), device_id_type=MESH)
-        return carry
+    late = (lax.rem(date, DEPTH) >= NEAR).astype(jnp.int32)
+    early_devices = 2 * NEAR * (groups // DEPTH)
+    alike = jnp.where(core == 0, early_devices, 2 * groups - early_devices)
+
+    def signal(semaphore, target):
+        pl.semaphore_signal(semaphore, inc=1, device_id=target, device_id_type=MESH)
 
     load_strip = pltpu.make_async_copy(slc_ref, strip, strip_sem)
     load_strip.start()
     load_table = pltpu.make_async_copy(offsets_ref, table, table_sem)
     load_table.start()
+
+    def greet(step, carry):
+        signal(barrier, (lax.rem(date + step, groups), late))
+        return carry
+
     lax.fori_loop(1, groups, greet, 0)
 
-    @pl.when(jnp.logical_not(own))
+    @pl.when(late != core)
     def _():
         greet(0, 0)
 
+    @pl.when(late == core)
+    def _():
+        signal(barrier, (date, 1 - core))
 
     load_strip.wait()
     lane = lax.broadcasted_iota(jnp.int32, (8, 128), 1)
@@ -178,10 +193,14 @@
 
     lax.fori_loop(0, chunks // 8, regroup, 0, unroll=8)
 
-    pl.semaphore_wait(barrier, jnp.where(own, chunks - 1, chunks))
-
-    def send(step, carry):
-        y, z, x = lax.rem(step // 2, 4), lax.rem(step // 8, DEPTH), step // (8 * DEPTH)
+    def count():
+        pl.semaphore_wait(barrier, jnp.where(late == core, alike - 1, alike + 1))
+        signal(other, (date, 1 - core))
+
+    def send(step, which):
+        depth = (NEAR, DEPTH - NEAR)[which]
+        first = (0, NEAR)[which]
+        z, y, x = first + lax.rem(step // 2, depth), lax.rem(step // (2 * depth), 4), step // (8 * depth)
         chunk = ((x * 4 + y) * DEPTH + z) * 2 + lax.rem(step, 2)
         owner = owners * core + chunk // 2
         owner_core = lax.rem(chunk, 2)
@@ -202,9 +221,32 @@
         def _():
             pltpu.make_async_copy(outgoing.at[chunk], arrived.at[date], recv_sem).start()
 
-        return carry
-
-    lax.fori_loop(0, chunks, send, 0)
+    def send_all(which):
+        def body(step, carry):
+            send(step, which)
+            return carry
+
+        lax.fori_loop(0, 16 * (NEAR, DEPTH - NEAR)[which], body, 0)
+
+    @pl.when(core == 0)
+    def _():
+        count()
+
+    @pl.when(core == 1)
+    def _():
+        pl.semaphore_wait(other, 1)
+
+    send_all(0)
+
+    @pl.when(core == 0)
+    def _():
+        pl.semaphore_wait(other, 1)
+
+    @pl.when(core == 1)
+    def _():
+        count()
+
+    send_all(1)
 
     load_table.wait()
     pairs = pair_mask(table[...])
@@ -256,6 +298,7 @@
                 pltpu.SemaphoreType.DMA,
                 pltpu.SemaphoreType.DMA,
                 pltpu.SemaphoreType.DMA,
+                pltpu.SemaphoreType.REGULAR,
             ],
             compiler_params=pltpu.CompilerParams(
                 collective_id=0, has_side_effects=True, vmem_limit_bytes=VMEM_BYTES

time: 25.4 us -> 23.5 us (0.925)
  the two profiles are of different devices: /device:TPU:3 before, /device:TPU:195 now
where the time goes in v4:
time: 23.5 us; the launch traced here: 23.4 us
  Pallas kernels  22.8 us (97%)
  local copies, waits for them, and re-layouts  0.6 us (3%)
    pallas_call x1, Pallas kernels, on_device(): pl.pallas_call(functools.partial(kernel, groups), out_shape=jax.ShapeDtyp...  22.8 us
    unnamed x1, local copies, waits for them, and re-layouts  0.6 us

profile of v4, /device:TPU:195, one launch (start us, length us, event | category | flops | bytes accessed | tf_op | source)
XLA Modules:
  0.0 23.4 jit_solution(17702973917508914923)
XLA Ops:
  0.0 22.8 %shard_map.28 = f32[2,4,1,256]{3,2,1,0:T(1,128)S(1)} custom-call(bf16[2,2,16,2048]{3,2,1,0:T(8,128)(2,1)} %slc_ref.1, s32[24,256]{1,0:T(8,128)} %bitcast.1), custom_call_target="tpu_custom_call" | custom-call | tf_op jit(solution)/shard_map/pallas_call | solution.py:285
  22.8 0.6 %copy.4 = f32[2,4,1,256]{3,2,1,0:T(1,128)} copy(f32[2,4,1,256]{3,2,1,0:T(1,128)S(1)} %shard_map.28) | data formatting | bytes 16384

commit v5 on v4

--- a/solution.py
+++ b/solution.py
@@ -159,7 +159,10 @@
         signal(barrier, (lax.rem(date + step, groups), late))
         return carry
 
-    lax.fori_loop(1, groups, greet, 0)
+    rest = (groups - 1) % 16
+    for step in range(1, 1 + rest):
+        greet(step, 0)
+    lax.fori_loop(1 + rest, groups, greet, 0, unroll=16)
 
     @pl.when(late != core)
     def _():

time: 23.5 us -> 23.1 us (0.983)
  Pallas kernels: 22.8 us -> 22.5 us
    pallas_call x1, Pallas kernels: 22.8 us -> 22.5 us  [on_device(): pl.pallas_call(functools.partial(kernel, groups), out_shape=jax.ShapeDtyp...]
where the time goes in v5:
time: 23.1 us
  Pallas kernels  22.5 us (97%)
  local copies, waits for them, and re-layouts  0.6 us (3%)
    pallas_call x1, Pallas kernels, on_device(): pl.pallas_call(functools.partial(kernel, groups), out_shape=jax.ShapeDtyp...  22.5 us
    unnamed x1, local copies, waits for them, and re-layouts  0.6 us

profile of v5, /device:TPU:195, one launch (start us, length us, event | category | flops | bytes accessed | tf_op | source)
XLA Modules:
  0.0 23.1 jit_solution(1538333483030481605)
XLA Ops:
  0.0 22.5 %shard_map.28 = f32[2,4,1,256]{3,2,1,0:T(1,128)S(1)} custom-call(bf16[2,2,16,2048]{3,2,1,0:T(8,128)(2,1)} %slc_ref.1, s32[24,256]{1,0:T(8,128)} %bitcast.1), custom_call_target="tpu_custom_call" | custom-call | tf_op jit(solution)/shard_map/pallas_call | solution.py:288
  22.5 0.6 %copy.4 = f32[2,4,1,256]{3,2,1,0:T(1,128)} copy(f32[2,4,1,256]{3,2,1,0:T(1,128)S(1)} %shard_map.28) | data formatting | bytes 16384

commit v6 on v5

--- a/solution.py
+++ b/solution.py
@@ -293,10 +293,10 @@
             scratch_shapes=[
                 pltpu.VMEM(slc.shape, jnp.bfloat16),
                 pltpu.VMEM(partner_offsets.shape[::-1], jnp.int32),
-                pltpu.VMEM((chunks // 8, 64, 128), jnp.float32),
+                pltpu.VMEM((chunks // 8 + 1, 64, 128), jnp.float32),
                 pltpu.VMEM((chunks, 8, 128), jnp.bfloat16),
                 pltpu.VMEM((groups, 8, 128), jnp.bfloat16),
-                pltpu.VMEM((groups * 8 + 4 * dates, 128), jnp.float32),
+                pltpu.VMEM((groups * 8 + 4 * dates + 8, 128), jnp.float32),
                 pltpu.SemaphoreType.DMA,
                 pltpu.SemaphoreType.DMA,
                 pltpu.SemaphoreType.DMA,

time: 23.1 us -> 23.1 us (level)
  no operation moved by 1% of the time
where the time goes in v6:
time: 23.1 us
  Pallas kernels  22.5 us (97%)
  local copies, waits for them, and re-layouts  0.6 us (3%)
    pallas_call x1, Pallas kernels, on_device(): pl.pallas_call(functools.partial(kernel, groups), out_shape=jax.ShapeDtyp...  22.5 us
    unnamed x1, local copies, waits for them, and re-layouts  0.6 us

profile of v6, /device:TPU:195, one launch (start us, length us, event | category | flops | bytes accessed | tf_op | source)
XLA Modules:
  0.0 23.1 jit_solution(8051824066844429401)
XLA Ops:
  0.0 22.5 %shard_map.28 = f32[2,4,1,256]{3,2,1,0:T(1,128)S(1)} custom-call(bf16[2,2,16,2048]{3,2,1,0:T(8,128)(2,1)} %slc_ref.1, s32[24,256]{1,0:T(8,128)} %bitcast.1), custom_call_target="tpu_custom_call" | custom-call | tf_op jit(solution)/shard_map/pallas_call | solution.py:288
  22.5 0.6 %copy.4 = f32[2,4,1,256]{3,2,1,0:T(1,128)} copy(f32[2,4,1,256]{3,2,1,0:T(1,128)S(1)} %shard_map.28) | data formatting | bytes 16384

commit v7 on v6

--- a/solution.py
+++ b/solution.py
@@ -203,7 +203,7 @@
     def send(step, which):
         depth = (NEAR, DEPTH - NEAR)[which]
         first = (0, NEAR)[which]
-        z, y, x = first + lax.rem(step // 2, depth), lax.rem(step // (2 * depth), 4), step // (8 * depth)
+        z, y, x = first + lax.rem(step // 2 + which * core, depth), lax.rem(step // (2 * depth), 4), step // (8 * depth)
         chunk = ((x * 4 + y) * DEPTH + z) * 2 + lax.rem(step, 2)
         owner = owners * core + chunk // 2
         owner_core = lax.rem(chunk, 2)

time: 23.1 us -> 23.1 us (level)
  no operation moved by 1% of the time
where the time goes in v7:
time: 23.1 us; the launch traced here: 23 us
  Pallas kernels  22.4 us (97%)
  local copies, waits for them, and re-layouts  0.6 us (3%)
    pallas_call x1, Pallas kernels, on_device(): pl.pallas_call(functools.partial(kernel, groups), out_shape=jax.ShapeDtyp...  22.4 us
    unnamed x1, local copies, waits for them, and re-layouts  0.6 us

profile of v7, /device:TPU:195, one launch (start us, length us, event | category | flops | bytes accessed | tf_op | source)
XLA Modules:
  0.0 23.0 jit_solution(5505591546641742849)
XLA Ops:
  0.0 22.4 %shard_map.28 = f32[2,4,1,256]{3,2,1,0:T(1,128)S(1)} custom-call(bf16[2,2,16,2048]{3,2,1,0:T(8,128)(2,1)} %slc_ref.1, s32[24,256]{1,0:T(8,128)} %bitcast.1), custom_call_target="tpu_custom_call" | custom-call | tf_op jit(solution)/shard_map/pallas_call | solution.py:288
  22.4 0.6 %copy.4 = f32[2,4,1,256]{3,2,1,0:T(1,128)} copy(f32[2,4,1,256]{3,2,1,0:T(1,128)S(1)} %shard_map.28) | data formatting | bytes 16384
